TPU v7x, 128 devices: a whole 4x4x4 slice. The times are simulated.
128 devices in a mesh: emit: 8 (over x_hi, z), elem: 16 (over y, x_lo, core).
Axes of the slice: x: 4 (x_hi: 2, x_lo: 2; x = x_hi * 2 + x_lo), y: 4, z: 4, core: 2. Of those that a mesh axis runs over, the one named last changes fastest.
Arguments:
- traces: float32 [256, 1024, 1024], P('emit', 'elem'), may hold values from -6 to 6
- codes: float32 [4, 2, 128], replicated, may hold values from -0.5 to 0.5
- code_of: int32 [256], replicated, may hold values from 0 to 3
- order: int32 [256], replicated, may hold values from 0 to 255, each once
- steer: float32 [256, 1024, 256], P(None, 'elem'), may hold values from -0.1875 to 0.1875
Outputs:
- beams: float32 [256, 256, 256], P('elem', 'emit')
Inputs may be any that keep to these rules, and one draw needn't show every extreme that they name: `order`: each value 0 to 255 appears exactly once.
All inputs are finite; a program needn't handle non-finite values.
Results may differ from a plain program's by a relative error of at most 0.000071.
Values sent between devices are 32-bit elements; how exact they have to be, the bound alone decides.
A program may use at most 192 MiB of HBM per device.

v0:
```python
import jax
import jax.numpy as jnp
from jax import lax
from jax.sharding import PartitionSpec as P


def toeplitz_table(codes):
    taps = codes.shape[2]
    rows = jnp.arange(2 * taps, dtype=jnp.int32)[:, None]
    cols = jnp.arange(taps, dtype=jnp.int32)[None, :]
    offset = rows - cols
    inside = (offset >= 0) & (offset < taps)
    clipped = jnp.clip(offset, 0, taps - 1)
    in_phase = jnp.where(inside[None], codes[:, 0, :][:, clipped], 0.0)
    quadrature = jnp.where(inside[None], codes[:, 1, :][:, clipped], 0.0)
    return jnp.concatenate([in_phase, quadrature], axis=2)


def hadamard_signs(order, columns, emissions):
    parity = jnp.zeros((order.shape[0], columns.shape[0]), jnp.int32)
    for bit in range(emissions.bit_length()):
        parity = parity + (order[:, None] >> bit & columns[None, :] >> bit & 1)
    signs = (1 - 2 * (parity % 2)).astype(jnp.float32)
    return signs / jnp.sqrt(jnp.float32(emissions))


def spectral_table(samples, taps, bins):
    rows = jnp.arange(samples // taps * 2 * taps, dtype=jnp.int32)
    block = rows // (2 * taps)
    quad = rows // taps % 2
    sample = block * taps + rows % taps
    freqs = jnp.arange(bins, dtype=jnp.int32) - bins // 2
    phase = jnp.mod(sample[:, None] * freqs[None, :], samples).astype(jnp.float32)
    angle = phase * (2.0 * jnp.pi / samples)
    cosine = jnp.cos(angle)
    sine = jnp.sin(angle)
    is_quad = quad[:, None] == 1
    real_cols = jnp.where(is_quad, sine, cosine)
    imag_cols = jnp.where(is_quad, cosine, -sine)
    return jnp.concatenate([real_cols, imag_cols], axis=1) / jnp.sqrt(jnp.float32(samples))


def steer_bins(source, steer, count, contract):
    bins = steer.shape[0]
    half = steer.shape[2] // 2
    real_part = lax.slice_in_dim(source, 0, count, axis=0)
    imag_part = lax.dynamic_slice_in_dim(source, bins, count, 0)
    numbers = (((contract,), (1,)), ((0,), (0,)))
    first = lax.dot_general(real_part, steer, numbers, precision=lax.Precision.HIGHEST)
    second = lax.dot_general(imag_part, steer, numbers, precision=lax.Precision.HIGHEST)
    return jnp.concatenate(
        [first[..., :half] - second[..., half:], first[..., half:] + second[..., :half]], axis=2
    )


def per_device(traces, codes, code_of, order, steer):
    edev, mdev, samples = traces.shape
    ncode, taps = (codes.shape[0], codes.shape[2])
    emissions = order.shape[0]
    bins = steer.shape[0]
    bins_dev = bins // lax.axis_size("elem")
    nblock = samples // taps
    first = lax.axis_index("emit") * edev
    own_codes = lax.dynamic_slice_in_dim(code_of, first, edev)
    onehot = (own_codes[:, None] == jnp.arange(ncode, dtype=jnp.int32)[None, :]).astype(jnp.float32)
    table = toeplitz_table(codes)
    picked = jnp.einsum("ec,cjd->ejd", onehot, table, precision=lax.Precision.HIGHEST)
    blocks = traces.reshape(edev, mdev, nblock, taps)
    current = jnp.einsum(
        "emnj,ejd->emnd", blocks, picked[:, :taps, :], precision=lax.Precision.HIGHEST
    )
    following = jnp.einsum(
        "emnj,ejd->emnd", blocks, picked[:, taps:, :], precision=lax.Precision.HIGHEST
    )
    following = jnp.concatenate(
        [following[:, :, 1:], jnp.zeros((edev, mdev, 1, 2 * taps), jnp.float32)], axis=2
    )
    corr = (current + following).reshape(edev, mdev, nblock * 2 * taps)
    transform = spectral_table(samples, taps, bins)
    spectra = lax.dot_general(
        transform, corr, (((0,), (2,)), ((), ())), precision=lax.Precision.HIGHEST
    )
    columns = first + jnp.arange(edev, dtype=jnp.int32)
    hadamard = hadamard_signs(order, columns, emissions)
    decoded = lax.dot_general(
        lax.all_gather(spectra, "emit", axis=1, tiled=True),
        hadamard,
        (((1,), (0,)), ((), ())),
        precision=lax.Precision.HIGHEST,
    )
    return lax.psum_scatter(
        steer_bins(decoded, steer, bins_dev * lax.axis_size("elem"), 1),
        "elem",
        scatter_dimension=0,
        tiled=True,
    )


def solution(mesh):
    placed = (P("emit", "elem", None), P(), P(), P(), P(None, "elem", None))
    return jax.shard_map(
        per_device, mesh=mesh, in_specs=placed, out_specs=P("elem", "emit", None), check_vma=False
    )
```

profile of v0, /device:TPU:0, one launch (start us, length us, event | category | flops | bytes accessed | tf_op | source)
XLA Modules:
  0.0 918.1 jit_solution(17875614214764076729)
XLA Ops:
  6.5 0.0 all-gather.2.cloned.1.call-start
  6.5 0.1 fusion.23
  6.7 0.8 fusion.93
  7.5 0.1 copy.40
  7.6 108.5 %gather_fusion = f32[32768,4]{1,0:T(8,128)} fusion(f32[4,128]{0,1:T(8,128)S(1)} %bitcast.52, s32[32768]{0:T(1024)S(1)} %fusion.23), kind=kCustom, calls=%fused_computation | custom fusion | bytes 1179648 | tf_op jit(solution)/shard_map/gather | solution.py:14
  116.0 9.4 %copy.16 = f32[256,128,4]{1,2,0:T(4,128)S(1)} copy(f32[256,128,4]{2,1,0:T(8,128)} %bitcast.56) | data formatting | bytes 1048576 | tf_op jit(solution)/shard_map/gather | solution.py:14
  125.5 0.1 copy.41
  125.6 108.5 %gather_fusion.1 = f32[32768,4]{1,0:T(8,128)} fusion(f32[4,128]{0,1:T(8,128)S(1)} %bitcast.51, s32[32768]{0:T(1024)S(1)} %fusion.23), kind=kCustom, calls=%fused_computation.1 | custom fusion | bytes 1179648 | tf_op jit(solution)/shard_map/gather | solution.py:15
  234.1 0.0 copy-start.2
  234.1 9.4 %copy.19 = f32[256,128,4]{1,2,0:T(4,128)S(1)} copy(f32[256,128,4]{2,1,0:T(8,128)} %bitcast.55) | data formatting | bytes 1048576 | tf_op jit(solution)/shard_map/gather | solution.py:15
  243.5 0.0 copy-done.2
  243.5 0.1 dynamic_slice.6
  243.6 0.3 select_bitcast_fusion.1
  243.9 0.0 slice-start
  243.9 5.9 fusion.15
  249.8 0.0 slice-start.1
  249.8 6.8 slice_bitcast_fusion.1
  256.6 0.0 slice-done
  256.6 0.0 slice-done.1
  256.6 17.6 %convolution_bitcast_fusion = f32[32,64,8,256]{3,1,2,0:T(8,128)} fusion(f32[32,128,256,1]{2,0,1,3:T(8,128)S(1)} %get-tuple-element.8, f32[32,64,1024]{2,1,0:T(8,128)S(1)} %bitcast.54), kind=kOutput, calls=%fused_computation.3 | convolution fusion | flops 6442450944 | bytes 29360128 | tf_op jit(solution)/shard_map/emnj,ejd->emnd/dot_general | solution.py:72
  274.2 13.1 %slice.46 = f32[32,64,7,256]{3,1,2,0:T(8,128)} slice(f32[32,64,8,256]{3,1,2,0:T(8,128)} %convolution_bitcast_fusion), slice={[0:32], [0:64], [1:8], [0:256]} | slice | bytes 29360128 | tf_op jit(solution)/shard_map/slice | solution.py:76
  287.3 29.1 %bitcast_add_fusion = f32[32,64,8,256]{3,1,2,0:T(8,128)} fusion(f32[32,64,7,256]{3,1,2,0:T(8,128)} %slice.46, f32[32,128,256,1]{2,0,1,3:T(8,128)} %get-tuple-element.7, f32[32,64,1024]{2,1,0:T(8,128)} %param.5), kind=kOutput, calls=%fused_computation.2 | convolution fusion | flops 6446645248 | bytes 44040192 | tf_op jit(solution)/shard_map/emnj,ejd->emnd/dot_general | solution.py:69
  316.4 18.2 %copy.38 = f32[32,64,8,256]{3,2,0,1:T(8,128)} copy(f32[32,64,8,256]{3,1,2,0:T(8,128)} %bitcast_add_fusion) | data formatting | bytes 33554432 | tf_op jit(solution)/shard_map/reshape | solution.py:78
  334.6 18.0 %reshape.181 = f32[32,64,2048]{2,0,1:T(8,128)} reshape(f32[32,64,8,256]{3,2,0,1:T(8,128)} %copy.38) | data formatting | bytes 33554432 | tf_op jit(solution)/shard_map/reshape | solution.py:78
  352.5 8.5 fusion.21
  361.1 30.8 %fusion.5 = f32[512,32,64]{0,1,2:T(8,128)} fusion(f32[32,64,2048]{2,0,1:T(8,128)} %reshape.181, f32[2048,256]{1,0:T(8,128)S(1)} %get-tuple-element.14, f32[2048,256]{1,0:T(8,128)S(1)} %get-tuple-element.13), kind=kOutput, calls=%fused_computation.15 | convolution fusion | flops 25771900928 | bytes 25165824 | tf_op jit(solution)/shard_map/dot_general | solution.py:80
  391.8 0.0 copy-start.1
  391.8 0.0 all-gather.2.cloned.1.call-update
  391.9 0.0 reduce-scatter.2.cloned.1.call-start
  392.0 0.5 copy-done.1
  392.5 336.3 %all-gather.2.cloned.1.call-done = f32[512,256,64]{0,1,2:T(8,128)} async-done(((f32[512,32,64]{0,1,2:T(8,128)}), f32[512,256,64]{0,1,2:T(8,128)}) %all-gather.2.cloned.1.call-update) | async-done | bytes 33554448 | tf_op jit(solution)/shard_map/all_gather | solution.py:86
  728.8 25.7 %fusion.33 = f32[512,64,32]{0,2,1:T(8,128)} fusion(f32[512,256,64]{0,1,2:T(8,128)} %all-gather.2.cloned.1.call-done, s32[32]{0:T(128)S(1)} %get-tuple-element.26, s32[256]{0:T(256)S(1)} %get-tuple-element.24, s32[32]{0:T(128)S(1)} %get-tuple-element.27, s32[256]{0:T(256)S(1)} %get-tuple-element.25, s32[32]{0:T(128)S(1)} %get-tuple-element.28, ...), kind=kOutput, calls=%fused_computation.55 | convolution fusion | flops 3221561344 | bytes 37759104 | tf_op jit(solution)/shard_map/dot_general | solution.py:85
  754.6 4.0 fusion.92
  758.6 5.6 copy.25
  764.2 4.5 copy.26
  768.6 0.0 copy-start
  768.7 16.0 %fusion.94 = f32[256,32,256]{2,1,0:T(8,128)} fusion(f32[256,64,32]{1,2,0:T(8,128)} %copy.25, f32[256,64,256]{2,1,0:T(8,128)} %param.9), kind=kOutput, calls=%fused_computation.136 | convolution fusion | flops 1610612736 | bytes 27262976 | tf_op jit(solution)/shard_map/dot_general | solution.py:49
  784.7 0.0 copy-done
  784.7 14.1 %fusion.95 = f32[256,32,256]{2,1,0:T(8,128)} fusion(f32[256,64,32]{1,2,0:T(8,128)S(1)} %copy-done, f32[256,64,256]{2,1,0:T(8,128)} %param.9), kind=kOutput, calls=%fused_computation.137 | convolution fusion | flops 1610612736 | bytes 27262976 | tf_op jit(solution)/shard_map/dot_general | solution.py:50
  798.8 9.9 %slice_subtract_fusion = (f32[256,32,128]{2,1,0:T(8,128)S(1)}, f32[256,32,128]{2,1,0:T(8,128)}) fusion(f32[256,32,256]{2,1,0:T(8,128)} %fusion.95, f32[256,32,256]{2,1,0:T(8,128)} %fusion.94), kind=kLoop, calls=%fused_computation.10 | loop fusion | flops 2097152 | bytes 25165824 | tf_op jit(solution)/shard_map/sub | solution.py:52
  808.7 6.4 pad_maximum_fusion
  815.1 0.0 reduce-scatter.2.cloned.1.call-update
  815.1 95.7 %reduce-scatter.2.cloned.1.call-done = f32[16,32,256]{2,1,0:T(8,128)} async-done(((f32[256,32,256]{2,1,0:T(8,128)}), f32[16,32,256]{2,1,0:T(8,128)}) %reduce-scatter.2.cloned.1.call-update) | async-done | bytes 524304 | tf_op jit(solution)/shard_map/reduce_scatter | solution.py:91
  (11 shorter events, 0.1 us)
Async XLA Ops:
  6.5 722.3 %all-gather.2.cloned.1.call-start = ((), (), s32[]{:S(2)}) async-start(), calls=%async_computation.1 | async-start | bytes 37748736 | tf_op jit(solution)/shard_map/all_gather | solution.py:86
  234.1 9.4 %copy-start.2 = (s32[256]{0:T(256)S(1)}, s32[256]{0:T(256)}, u32[]{:S(2)}) copy-start(s32[256]{0:T(256)} %param.7) | copy-start | bytes 3076
  243.9 12.7 %slice-start = ((s8[8388608]{0:T(1024)(128)(4,1)}), s8[4194304]{0:T(1024)(128)(4,1)S(1)}, s32[]{:S(2)}) async-start(s8[8388608]{0:T(1024)(128)(4,1)} %bitcast.53), calls=%async_computation.3 | async-start | bytes 8388608
  249.8 6.8 slice-start.1
  391.8 0.7 copy-start.1
  391.9 518.9 %reduce-scatter.2.cloned.1.call-start = ((), (), s32[]{:S(2)}) async-start(), calls=%async_computation.2 | async-start | bytes 8912896 | tf_op jit(solution)/shard_map/reduce_scatter | solution.py:91
  768.6 16.0 %copy-start = (f32[256,64,32]{1,2,0:T(8,128)S(1)}, f32[256,64,32]{1,2,0:T(8,128)}, u32[]{:S(2)}) copy-start(f32[256,64,32]{1,2,0:T(8,128)} %copy.26) | copy-start | bytes 6291460
Sparse Core Ops, SparseCore 0:
  392.0 336.7 all-gather.1
  815.2 95.5 reduce-scatter.1
where the time goes:
time: 926 us; the launch traced here: 918 us
  waiting for transfers between devices  432 us (47%)
  local copies, waits for them, and re-layouts  308 us (33%)
  matrix products  139 us (15%)
  other arithmetic  25.2 us (3%)
  between operations  14 us (2%)
    all_gather x1, waiting for transfers between devices, per_device(): lax.all_gather(spectra, 'emit', axis=1, tiled=True)  336 us
    gather x2, local copies, waits for them, and re-layouts, toeplitz_table(): quadrature = jnp.where(inside[None], codes[:, 1, :][:, clipped], 0.0)  118 us
    gather x2, local copies, waits for them, and re-layouts, toeplitz_table(): in_phase = jnp.where(inside[None], codes[:, 0, :][:, clipped], 0.0)  118 us
    reduce_scatter x1, waiting for transfers between devices, per_device(): lax.psum_scatter(steer_bins(decoded, steer, bins_dev * lax.axis_size('ele...  95.7 us
    reshape x2, local copies, waits for them, and re-layouts, per_device(): corr = (current + following).reshape(edev, mdev, nblock * 2 * taps)  36.1 us
    dot_general x1, matrix products, per_device(): lax.dot_general(transform, corr, (((0,), (2,)), ((), ())), precision=lax....  30.8 us
    dot_general x1, matrix products, per_device(): jnp.einsum('emnj,ejd->emnd', blocks, picked[:, :taps, :], precision=lax.P...  29.1 us
    dot_general x1, matrix products, per_device(): lax.dot_general(lax.all_gather(spectra, 'emit', axis=1, tiled=True), hada...  25.7 us
  transfers between devices with their start and end apart: 2, of which 2 were waited for; matrix products, arithmetic and copies ran while one was open for 0% of the time, Pallas kernels for 0%

commit v1 on v0

v1 whole, which is shorter than its diff:
```python
import functools
import numpy as np
import jax
import jax.numpy as jnp
from jax import lax
from jax.experimental import pallas as pl
from jax.experimental.pallas import tpu as pltpu

from jax.sharding import PartitionSpec as P

HIGH = lax.Precision.HIGH
NT = (((1,), (1,)), ((), ()))


def dft_tables(samples, taps, half):
    t = np.arange(taps, samples)
    pos = np.arange(half)
    cosine = np.cos(2 * np.pi * (pos[:, None] * t[None] % samples) / samples)
    sine = np.sin(2 * np.pi * (pos[:, None] * t[None] % samples) / samples)
    top = 2 * np.pi * (half * t % samples) / samples
    sine[0] = np.cos(top)
    extra = np.zeros((8, t.size))
    extra[0] = np.sin(top)
    body = np.concatenate([cosine, sine, extra], 0).astype(np.float32)
    freq = np.concatenate([pos, np.where(pos == 0, -half, -pos)])
    u = np.arange(taps)
    angle = 2 * np.pi * (freq[:, None] * u[None] % samples) / samples
    head = np.stack([np.cos(angle), np.sin(angle)]).astype(np.float32)
    tri = (u[:, None] <= u[None, :]).astype(np.float32)
    return body, head, tri


def spectra_kernel(scale, code_ref, codes_ref, head_ref, tri_ref, body_ref, x_ref, out_ref, gain_ref, tab_ref):
    step = pl.program_id(0)
    ncode, _, taps = codes_ref.shape
    eblk, mdev, samples = x_ref.shape
    half = out_ref.shape[1]
    nrow = 2 * half

    @pl.when(step == 0)
    def _():
        cosine, sine = head_ref[0], head_ref[1]
        for c in range(ncode):
            ci = codes_ref[c, 0:1, :] * scale
            cq = codes_ref[c, 1:2, :] * scale
            a_re = ci * cosine - cq * sine
            a_im = ci * sine + cq * cosine
            p_re = jnp.dot(a_re, tri_ref[...], precision=lax.Precision.HIGHEST, preferred_element_type=jnp.float32)
            p_im = jnp.dot(a_im, tri_ref[...], precision=lax.Precision.HIGHEST, preferred_element_type=jnp.float32)
            lanes = slice(c * taps, (c + 1) * taps)
            gain_ref[0:nrow, lanes] = cosine * p_re + sine * p_im
            gain_ref[nrow:, lanes] = cosine * p_im - sine * p_re
            tab_ref[c, 0:nrow] = jnp.broadcast_to(p_re[:, taps - 1:], (nrow, 128))
            tab_ref[c, nrow:] = jnp.broadcast_to(p_im[:, taps - 1:], (nrow, 128))

    x = x_ref[...].reshape(eblk * mdev, samples)
    spec = lax.dot_general(body_ref[...], x[:, taps:], NT, precision=HIGH, preferred_element_type=jnp.float32)
    codes = [code_ref[step * eblk + e] for e in range(eblk)]
    masked = jnp.concatenate(
        [
            jnp.concatenate(
                [x_ref[e, :, 0:taps] * (codes[e] == c).astype(jnp.float32) for e in range(eblk)], axis=0
            )
            for c in range(ncode)
        ],
        axis=1,
    )
    corr = lax.dot_general(gain_ref[...], masked, NT, precision=HIGH, preferred_element_type=jnp.float32)
    first = lax.broadcasted_iota(jnp.int32, (half, 128), 0) == 0
    left = lax.broadcasted_iota(jnp.int32, (half, 128), 1) < mdev
    for sign in range(2):
        rows = slice(sign * half, (sign + 1) * half)
        irows = slice(nrow + sign * half, nrow + (sign + 1) * half)
        planes = []
        for q in range(eblk // 2):
            lanes = slice(q * 128, (q + 1) * 128)
            xc, xs = spec[0:half, lanes], spec[half:nrow, lanes]
            cr = jnp.where(left, tab_ref[codes[2 * q], rows], tab_ref[codes[2 * q + 1], rows])
            ci = jnp.where(left, tab_ref[codes[2 * q], irows], tab_ref[codes[2 * q + 1], irows])
            if sign == 0:
                xs = jnp.where(first, 0.0, -xs)
            else:
                xc = jnp.where(first, xs, xc)
                xs = jnp.where(first, spec[nrow:nrow + 1, lanes], xs)
            re = xc * cr - xs * ci + corr[rows, lanes]
            im = xc * ci + xs * cr + corr[irows, lanes]
            planes.append(jnp.where(left, re, pltpu.roll(im, 64, 1)))
            planes.append(jnp.where(left, pltpu.roll(re, 64, 1), im))
        out_ref[sign] = jnp.swapaxes(jnp.stack(planes, 0), 0, 1)


def spectra(traces, codes, own_codes, nb=256):
    edev, mdev, samples = traces.shape
    ncode, _, taps = codes.shape
    half = nb // 2
    body, head, tri = dft_tables(samples, taps, half)
    eblk = 8
    full = lambda s: pl.BlockSpec(s, lambda i: (0,) * len(s))
    return pl.pallas_call(
        functools.partial(spectra_kernel, float(samples) ** -0.5),
        grid=(edev // eblk,),
        in_specs=[
            pl.BlockSpec(memory_space=pltpu.SMEM),
            full(codes.shape), full(head.shape), full(tri.shape), full(body.shape),
            pl.BlockSpec((eblk, mdev, samples), lambda i: (i, 0, 0)),
        ],
        out_specs=pl.BlockSpec((2, half, eblk, 2 * mdev), lambda i: (0, 0, i, 0)),
        out_shape=jax.ShapeDtypeStruct((2, half, edev, 2 * mdev), jnp.float32),
        scratch_shapes=[
            pltpu.VMEM((4 * half, ncode * taps), jnp.float32),
            pltpu.VMEM((ncode, 4 * half, 128), jnp.float32),
        ],
        compiler_params=pltpu.CompilerParams(vmem_limit_bytes=56 << 20),
        name="spectra",
    )(own_codes, codes, head, tri, body, traces)


def steer_kernel(d_ref, s_ref, out_ref):
    step = pl.program_id(0)
    blk, mdev, width = s_ref.shape
    half = d_ref.shape[1]
    lines = width // 2

    def one(k, carry):
        b = step * blk + k
        sign = 1 - b // half
        row = (b - half) * (1 - 2 * sign)
        row = lax.rem(row, half)
        d = d_ref[sign, row]
        s = s_ref[k]
        w = jnp.concatenate([s, jnp.concatenate([-s[:, lines:], s[:, :lines]], axis=1)], axis=0)
        out_ref[k] = jnp.dot(d, w, precision=HIGH, preferred_element_type=jnp.float32)
        return carry

    lax.fori_loop(0, blk, one, 0, unroll=True)


def steered(decoded, steer):
    bins, mdev, width = steer.shape
    edev = decoded.shape[2]
    blk = 16
    return pl.pallas_call(
        steer_kernel,
        grid=(bins // blk,),
        in_specs=[
            pl.BlockSpec(decoded.shape, lambda i: (0, 0, 0, 0)),
            pl.BlockSpec((blk, mdev, width), lambda i: (i, 0, 0)),
        ],
        out_specs=pl.BlockSpec((blk, edev, width), lambda i: (i, 0, 0)),
        out_shape=jax.ShapeDtypeStruct((bins, edev, width), jnp.float32),
        compiler_params=pltpu.CompilerParams(vmem_limit_bytes=56 << 20),
        name="steer",
    )(decoded, steer)


def hadamard_signs(order, columns):
    both = order[:, None] & columns[None, :]
    parity = lax.population_count(both) & 1
    return (1 - 2 * parity).astype(jnp.float32) / jnp.sqrt(jnp.float32(order.shape[0]))


def per_device(traces, codes, code_of, order, steer):
    edev = traces.shape[0]
    emissions = order.shape[0]
    first = lax.axis_index("emit") * edev
    own_codes = lax.dynamic_slice_in_dim(code_of, first, edev)
    spec = spectra(traces, codes, own_codes, steer.shape[0])
    part = steered(spec, steer)
    summed = lax.psum_scatter(part, "elem", scatter_dimension=0, tiled=True)
    gathered = lax.all_to_all(summed, "emit", 0, 1, tiled=True)
    hadamard = hadamard_signs(order, jnp.arange(emissions, dtype=jnp.int32))
    decoded = jnp.einsum("ek,bel->bkl", hadamard, gathered, precision=lax.Precision.HIGHEST)
    return lax.all_to_all(decoded, "emit", 1, 0, tiled=True)


def solution(mesh):
    placed = (P("emit", "elem", None), P(), P(), P(), P(None, "elem", None))
    return jax.shard_map(
        per_device, mesh=mesh, in_specs=placed, out_specs=P("elem", "emit", None), check_vma=False
    )
```

time: 926 us -> 180 us (0.19)
  waiting for transfers between devices: 432 us -> 100 us
  local copies, waits for them, and re-layouts: 308 us -> 2.4 us
  matrix products: 139 us -> 1.07 us
  Pallas kernels: 0 us -> 32.1 us
  blocking collectives: 0 us -> 29.4 us
  other arithmetic: 25.2 us -> 0 us
    all_gather x1 -> x0, waiting for transfers between devices: 336 us -> none  [per_device(): lax.all_gather(spectra, 'emit', axis=1, tiled=True)]
    gather x4 -> x0, local copies, waits for them, and re-layouts: 236 us -> none  [the longest x2 118 us: toeplitz_table(): quadrature = jnp.where(inside[None], codes[:, 1, :][:, clipped], 0.0)]
    dot_general x7 -> x1, matrix products: 139 us -> 1.07 us  [per_device(): jnp.einsum('ek,bel->bkl', hadamard, gathered, precision=lax.Precision.HIG...]
    reshape x2 -> x0, local copies, waits for them, and re-layouts: 36.1 us -> none  [per_device(): corr = (current + following).reshape(edev, mdev, nblock * 2 * taps)]
    pallas_call x0 -> x2, Pallas kernels: none -> 32.1 us  [the longest x1 18.8 us: steered(): pl.pallas_call(steer_kernel, grid=(bins // blk,), in_specs=[pl.BlockSpec(...]
    slice x5 -> x0, local copies, waits for them, and re-layouts: 30.3 us -> none  [the longest x1 13.1 us: per_device(): following[:, :, 1:]]
    all_to_all x0 -> x2, blocking collectives: none -> 29.4 us  [the longest x1 16.7 us: per_device(): gathered = lax.all_to_all(summed, 'emit', 0, 1, tiled=True)]
    sub x2 -> x0, other arithmetic: 9.89 us -> none  [the longest x1 9.88 us: steer_bins(): first[..., :half] - second[..., half:]]
  transfers between devices with their start and end apart: 2 -> 1, of which waited for: 2 -> 1; matrix products, arithmetic and copies ran while one was open for 0% -> 0% of each run, Pallas kernels for 0% -> 0%
where the time goes in v1:
time: 180 us; the launch traced here: 179 us
  waiting for transfers between devices  100 us (56%)
  Pallas kernels  32.1 us (18%)
  blocking collectives  29.4 us (16%)
  between operations  13.4 us (7%)
  local copies, waits for them, and re-layouts  2.4 us (1%)
    reduce_scatter x1, waiting for transfers between devices, per_device(): summed = lax.psum_scatter(part, 'elem', scatter_dimension=0, tiled=True)  100 us
    pallas_call x1, Pallas kernels, steered(): pl.pallas_call(steer_kernel, grid=(bins // blk,), in_specs=[pl.BlockSpec(...  18.8 us
    all_to_all x1, blocking collectives, per_device(): gathered = lax.all_to_all(summed, 'emit', 0, 1, tiled=True)  16.7 us
    pallas_call x1, Pallas kernels, spectra(): pl.pallas_call(functools.partial(spectra_kernel, float(samples) ** (-0.5)...  13.4 us
    all_to_all x1, blocking collectives, per_device(): return lax.all_to_all(decoded, 'emit', 1, 0, tiled=True)  12.7 us
  transfers between devices with their start and end apart: 1, of which 1 were waited for; matrix products, arithmetic and copies ran while one was open for 0% of the time, Pallas kernels for 0%

profile of v1, /device:TPU:0, one launch (start us, length us, event | category | flops | bytes accessed | tf_op | source)
XLA Modules:
  0.0 178.8 jit_solution(4877096091338744904)
XLA Ops:
  6.5 0.0 reduce-scatter.2.cloned.1.call-start
  6.5 1.3 dynamic_slice.3.code_ref
  7.8 13.4 %spectra.1.d_ref = f32[2,128,32,128]{3,2,1,0:T(8,128)} custom-call(s32[32]{0:T(128)} %dynamic_slice.3.code_ref, f32[4,2,128]{2,1,0:T(2,128)} %codes_ref.1, f32[2,256,128]{2,1,0:T(8,128)} %constant.25.clone.head_ref, f32[128,128]{1,0:T(8,128)} %constant.26.clone.tri_ref, f32[264,896]{1,0:T(8,128)} %constant.27.clone.body_ref, f32[32,64,1024]{2,1,0:T(8,128)} %x_ref.1), custom_call_target="tpu_custom_call" | custom-call | tf_op jit(solution)/shard_map/spectra/pallas_call | solution.py:99
  21.2 18.8 %steer.1 = f32[256,32,256]{2,1,0:T(8,128)} custom-call(f32[2,128,32,128]{3,2,1,0:T(8,128)} %spectra.1.d_ref, f32[256,64,256]{2,1,0:T(8,128)} %s_ref.1), custom_call_target="tpu_custom_call" | custom-call | tf_op jit(solution)/shard_map/steer/pallas_call | solution.py:142
  39.9 0.0 copy-start
  39.9 0.0 reduce-scatter.2.cloned.1.call-update
  40.0 100.4 %reduce-scatter.2.cloned.1.call-done = f32[16,32,256]{2,1,0:T(8,128)} async-done(((f32[256,32,256]{2,1,0:T(8,128)}), f32[16,32,256]{2,1,0:T(8,128)}) %reduce-scatter.2.cloned.1.call-update) | async-done | bytes 524304 | tf_op jit(solution)/shard_map/reduce_scatter | solution.py:169
  140.3 16.7 %all_to_all.36 = f32[16,32,256]{2,1,0:T(8,128)S(1)} all-to-all(f32[16,32,256]{2,1,0:T(8,128)} %reduce-scatter.2.cloned.1.call-done), channel_id=1, replica_groups=mesh['emit'=8,'elem'=16] {'emit'}, dimensions={0} | all-to-all | bytes 1048576 | tf_op jit(solution)/shard_map/all_to_all | solution.py:170
  157.1 0.0 copy-done
  157.1 1.1 convolution_bitcast_fusion
  158.2 0.2 copy.20
  158.4 12.7 %all_to_all.37 = f32[2,256,256]{2,0,1:T(2,128)S(1)} all-to-all(f32[2,256,256]{2,0,1:T(2,128)S(1)} %copy.20), channel_id=1, replica_groups=mesh['emit'=8,'elem'=16] {'emit'}, dimensions={1} | all-to-all | bytes 1048576 | tf_op jit(solution)/shard_map/all_to_all | solution.py:173
  171.2 0.8 copy.22
  (2 shorter events, 0.1 us)
Async XLA Ops:
  6.5 133.8 %reduce-scatter.2.cloned.1.call-start = ((), (), s32[]{:S(2)}) async-start(), calls=%async_computation.3 | async-start | bytes 8912896 | tf_op jit(solution)/shard_map/reduce_scatter | solution.py:169
  39.9 117.1 %copy-start = (s32[256]{0:T(256)S(1)}, s32[256]{0:T(256)}, u32[]{:S(2)}) copy-start(s32[256]{0:T(256)} %param.11) | copy-start | bytes 3076
Sparse Core Ops, SparseCore 0:
  40.1 100.2 reduce-scatter.1

commit v2 on v1

--- a/solution.py
+++ b/solution.py
@@ -115,62 +115,227 @@
     )(own_codes, codes, head, tri, body, traces)
 
 
-def steer_kernel(d_ref, s_ref, out_ref):
-    step = pl.program_id(0)
-    blk, mdev, width = s_ref.shape
-    half = d_ref.shape[1]
-    lines = width // 2
-
-    def one(k, carry):
-        b = step * blk + k
+MESH = pl.DeviceIdType.MESH
+ROUNDS = 16
+SLOT_Y = (2, 1, 2, 3, 1, 3, 0, 0)
+SLOT_X = (0, 1, 1, 0, 0, 1, 0, 1)
+
+
+def beam_kernel(
+    order_ref, d_ref, steer_ref, out_ref,
+    wbuf, sendc, recvc, acc, recv1, recv2, fwd, totx, recvx, fin, gath, dec, had,
+    wsem, csem, crsem, ysem, yrsem, y2sem, y2rsem, xsem, xrsem, asem, arsem, osem, orsem,
+):
+    i, j = lax.axis_index("emit"), lax.axis_index("elem")
+    y, x, c = j // 4, j // 2 % 2, j % 2
+    nemit = 8
+    half, edev = d_ref.shape[1], d_ref.shape[2]
+    lines = steer_ref.shape[3] // 2
+
+    def at(yy, xx, cc):
+        return (i, (yy * 2 + xx) * 2 + cc)
+
+    other_core = at(y, x, 1 - c)
+    up, down = at((y + 1) % 4, x, c), at((y + 3) % 4, x, c)
+    other_x = at(y, 1 - x, c)
+
+    def emit_peer(q):
+        return ((i + q) % nemit, j)
+
+    def bin_of(t):
+        return (i + t) % nemit * 2 + t // nemit
+
+    def remote(src, dst, ssem, rsem, device):
+        return pltpu.make_async_remote_copy(
+            src_ref=src, dst_ref=dst, send_sem=ssem, recv_sem=rsem, device_id=device, device_id_type=MESH
+        )
+
+    def load(t):
+        return pltpu.make_async_copy(steer_ref.at[:, bin_of(t)], wbuf.at[t % 4], wsem.at[t % 4])
+
+    def core_copy(t):
+        return remote(sendc.at[t], recvc.at[t], csem.at[t], crsem.at[t], other_core)
+
+    def y1_copy(t, d):
+        return remote(acc.at[t, pl.ds(2 * d, 2)], recv1.at[t, d], ysem.at[t, d], yrsem.at[t, d], up if d == 0 else down)
+
+    def y2_copy(t, d):
+        return remote(fwd.at[t, d], recv2.at[t, d], y2sem.at[t, d], y2rsem.at[t, d], up if d == 0 else down)
+
+    def x_copy(t):
+        return remote(totx.at[t], recvx.at[t], xsem.at[t], xrsem.at[t], other_x)
+
+    def a_copy(t):
+        q = t % nemit
+        return remote(
+            fin.at[t], gath.at[t // nemit, pl.ds(pl.multiple_of(i * edev, edev), edev)], asem.at[t], arsem.at[t], emit_peer(q)
+        )
+
+    def o_copy(s, q):
+        k = (i + q) % nemit
+        return remote(
+            dec.at[s, pl.ds(pl.multiple_of(k * edev, edev), edev)], out_ref.at[2 * i + s], osem.at[s, q], orsem.at[s, q], emit_peer(q)
+        )
+
+    load(0).start()
+    load(1).start()
+    barrier = pltpu.get_barrier_semaphore()
+    peers = [other_core, up, down, other_x] + [emit_peer(q) for q in range(1, nemit)]
+    for peer in peers:
+        pl.semaphore_signal(barrier, inc=1, device_id=peer, device_id_type=MESH)
+    both = order_ref[...] & lax.broadcasted_iota(jnp.int32, had.shape, 0)
+    for shift in (4, 2, 1):
+        both = both ^ (both >> shift)
+    had[...] = ((1 - 2 * (both & 1)).astype(jnp.float32) * (had.shape[0] ** -0.5)).astype(jnp.bfloat16)
+    pl.semaphore_wait(barrier, len(peers))
+
+    def product(t, slot, core):
+        jj = ((y + SLOT_Y[slot]) % 4 * 2 + SLOT_X[slot]) * 2 + core
+        b = jj * 16 + bin_of(t)
         sign = 1 - b // half
-        row = (b - half) * (1 - 2 * sign)
-        row = lax.rem(row, half)
-        d = d_ref[sign, row]
-        s = s_ref[k]
+        row = (b - half) * (1 - 2 * sign) % half
+        s = wbuf[t % 4, jj]
         w = jnp.concatenate([s, jnp.concatenate([-s[:, lines:], s[:, :lines]], axis=1)], axis=0)
-        out_ref[k] = jnp.dot(d, w, precision=HIGH, preferred_element_type=jnp.float32)
+        return jnp.dot(d_ref[sign, row], w, precision=HIGH, preferred_element_type=jnp.float32)
+
+    def decode(s):
+        for q in range(1, nemit):
+            a_copy(s * nemit + q).wait_recv()
+        g = gath[s]
+        hi = g.astype(jnp.bfloat16)
+        lo = (g - hi.astype(jnp.float32)).astype(jnp.bfloat16)
+        h = had[...]
+        dec[s] = jnp.dot(h, hi, preferred_element_type=jnp.float32) + jnp.dot(h, lo, preferred_element_type=jnp.float32)
+        for q in range(1, nemit):
+            o_copy(s, q).start()
+        out_ref[2 * i + s] = dec[s, pl.ds(pl.multiple_of(i * edev, edev), edev)]
+
+    def body(t, carry):
+        @pl.when(t + 2 < ROUNDS)
+        def _():
+            load(t + 2).start()
+
+        @pl.when(t < ROUNDS)
+        def _():
+            load(t).wait()
+            for slot in range(8):
+                sendc[t, slot] = product(t, slot, 1 - c)
+            core_copy(t).start()
+
+        @pl.when((t >= 1) & (t < ROUNDS + 1))
+        def _():
+            u = t - 1
+            core_copy(u).wait_recv()
+            for slot in range(8):
+                acc[u, slot] = product(u, slot, c) + recvc[u, slot]
+                if slot == 1:
+                    y1_copy(u, 0).start()
+                if slot == 3:
+                    y1_copy(u, 1).start()
+
+        @pl.when((t >= 2) & (t < ROUNDS + 2))
+        def _():
+            u = t - 2
+            for d in range(2):
+                y1_copy(u, d).wait_recv()
+                fwd[u, d] = acc[u, 4 + d] + recv1[u, d, 0]
+                y2_copy(u, d).start()
+
+        @pl.when((t >= 3) & (t < ROUNDS + 3))
+        def _():
+            u = t - 3
+            for d in range(2):
+                y2_copy(u, d).wait_recv()
+            tot0 = acc[u, 6] + recv2[u, 0] + recv1[u, 1, 1]
+            tot1 = acc[u, 7] + recv2[u, 1] + recv1[u, 0, 1]
+            mine = (x == 0).astype(jnp.float32)
+            totx[u] = tot1 * mine + tot0 * (1.0 - mine)
+            fin[u] = tot0 * mine + tot1 * (1.0 - mine)
+            x_copy(u).start()
+
+        @pl.when((t >= 4) & (t < ROUNDS + 4))
+        def _():
+            u = t - 4
+            x_copy(u).wait_recv()
+            fin[u] = fin[u] + recvx[u]
+
+            @pl.when(u % nemit == 0)
+            def _():
+                gath[u // nemit, pl.ds(pl.multiple_of(i * edev, edev), edev)] = fin[u]
+
+            @pl.when(u % nemit != 0)
+            def _():
+                a_copy(u).start()
+
+        @pl.when(t == nemit + 5)
+        def _():
+            decode(0)
+
         return carry
 
-    lax.fori_loop(0, blk, one, 0, unroll=True)
-
-
-def steered(decoded, steer):
+    lax.fori_loop(0, ROUNDS + 4, body, 0)
+    decode(1)
+
+    def drain(t, carry):
+        core_copy(t).wait_send()
+        for d in range(2):
+            y1_copy(t, d).wait_send()
+            y2_copy(t, d).wait_send()
+        x_copy(t).wait_send()
+
+        @pl.when(t % nemit != 0)
+        def _():
+            a_copy(t).wait_send()
+
+        return carry
+
+    lax.fori_loop(0, ROUNDS, drain, 0)
+    for s in range(2):
+        for q in range(1, nemit):
+            o_copy(s, q).wait()
+
+
+def beams(order, spec, steer):
     bins, mdev, width = steer.shape
-    edev = decoded.shape[2]
-    blk = 16
+    edev = spec.shape[2]
+    emissions = order.shape[0]
+    block = (edev, width)
+    f32 = jnp.float32
+    dma = pltpu.SemaphoreType.DMA
+    vmem = pl.BlockSpec(memory_space=pltpu.VMEM)
     return pl.pallas_call(
-        steer_kernel,
-        grid=(bins // blk,),
-        in_specs=[
-            pl.BlockSpec(decoded.shape, lambda i: (0, 0, 0, 0)),
-            pl.BlockSpec((blk, mdev, width), lambda i: (i, 0, 0)),
+        beam_kernel,
+        in_specs=[vmem, vmem, pl.BlockSpec(memory_space=pl.ANY)],
+        out_specs=vmem,
+        out_shape=jax.ShapeDtypeStruct((16, edev, width), f32),
+        scratch_shapes=[
+            pltpu.VMEM((4, 16, mdev, width), f32),
+            pltpu.VMEM((ROUNDS, 8) + block, f32),
+            pltpu.VMEM((ROUNDS, 8) + block, f32),
+            pltpu.VMEM((ROUNDS, 8) + block, f32),
+            pltpu.VMEM((ROUNDS, 2, 2) + block, f32),
+            pltpu.VMEM((ROUNDS, 2) + block, f32),
+            pltpu.VMEM((ROUNDS, 2) + block, f32),
+            pltpu.VMEM((ROUNDS,) + block, f32),
+            pltpu.VMEM((ROUNDS,) + block, f32),
+            pltpu.VMEM((ROUNDS,) + block, f32),
+            pltpu.VMEM((2, emissions, width), f32),
+            pltpu.VMEM((2, emissions, width), f32),
+            pltpu.VMEM((emissions, emissions), jnp.bfloat16),
+            dma((4,)), dma((ROUNDS,)), dma((ROUNDS,)), dma((ROUNDS, 2)), dma((ROUNDS, 2)), dma((ROUNDS, 2)), dma((ROUNDS, 2)),
+            dma((ROUNDS,)), dma((ROUNDS,)), dma((ROUNDS,)), dma((ROUNDS,)), dma((2, 8)), dma((2, 8)),
         ],
-        out_specs=pl.BlockSpec((blk, edev, width), lambda i: (i, 0, 0)),
-        out_shape=jax.ShapeDtypeStruct((bins, edev, width), jnp.float32),
-        compiler_params=pltpu.CompilerParams(vmem_limit_bytes=56 << 20),
-        name="steer",
-    )(decoded, steer)
-
-
-def hadamard_signs(order, columns):
-    both = order[:, None] & columns[None, :]
-    parity = lax.population_count(both) & 1
-    return (1 - 2 * parity).astype(jnp.float32) / jnp.sqrt(jnp.float32(order.shape[0]))
+        compiler_params=pltpu.CompilerParams(collective_id=0, has_side_effects=True, vmem_limit_bytes=60 << 20),
+        name="beams",
+    )(order.reshape(1, emissions), spec, steer.reshape(16, bins // 16, mdev, width))
 
 
 def per_device(traces, codes, code_of, order, steer):
     edev = traces.shape[0]
-    emissions = order.shape[0]
     first = lax.axis_index("emit") * edev
     own_codes = lax.dynamic_slice_in_dim(code_of, first, edev)
     spec = spectra(traces, codes, own_codes, steer.shape[0])
-    part = steered(spec, steer)
-    summed = lax.psum_scatter(part, "elem", scatter_dimension=0, tiled=True)
-    gathered = lax.all_to_all(summed, "emit", 0, 1, tiled=True)
-    hadamard = hadamard_signs(order, jnp.arange(emissions, dtype=jnp.int32))
-    decoded = jnp.einsum("ek,bel->bkl", hadamard, gathered, precision=lax.Precision.HIGHEST)
-    return lax.all_to_all(decoded, "emit", 1, 0, tiled=True)
+    return beams(order, spec, steer)
 
 
 def solution(mesh):

time: 180 us -> 92.9 us (0.52)
  waiting for transfers between devices: 100 us -> 0 us
  Pallas kernels: 32.1 us -> 89.6 us
  blocking collectives: 29.4 us -> 0 us
  between operations: 13.4 us -> 0.01 us
    reduce_scatter x1 -> x0, waiting for transfers between devices: 100 us -> none  [per_device(): summed = lax.psum_scatter(part, 'elem', scatter_dimension=0, tiled=True)]
    pallas_call x1, Pallas kernels: 18.8 us -> 76.2 us  [beams(): pl.pallas_call(beam_kernel, in_specs=[vmem, vmem, pl.BlockSpec(memory_spa...]
    all_to_all x2 -> x0, blocking collectives: 29.4 us -> none  [the longest x1 16.7 us: per_device(): gathered = lax.all_to_all(summed, 'emit', 0, 1, tiled=True)]
    unnamed x2 -> x1, local copies, waits for them, and re-layouts: 0.01 us -> 1.88 us
  transfers between devices with their start and end apart: 1 -> 0, of which waited for: 1 -> 0; matrix products, arithmetic and copies ran while one was open for 0% -> 0% of each run, Pallas kernels for 0% -> 0%
where the time goes in v2:
time: 92.9 us; the launch traced here: 92.7 us
  Pallas kernels  89.6 us (96%)
  local copies, waits for them, and re-layouts  3.14 us (3%)
    pallas_call x1, Pallas kernels, beams(): pl.pallas_call(beam_kernel, in_specs=[vmem, vmem, pl.BlockSpec(memory_spa...  76.2 us
    pallas_call x1, Pallas kernels, spectra(): pl.pallas_call(functools.partial(spectra_kernel, float(samples) ** (-0.5)...  13.3 us
    unnamed x1, local copies, waits for them, and re-layouts  1.88 us

profile of v2, /device:TPU:0, one launch (start us, length us, event | category | flops | bytes accessed | tf_op | source)
XLA Modules:
  0.0 92.7 jit_solution(1150978100708908107)
XLA Ops:
  0.0 1.3 %dynamic_slice.3.code_ref = s32[32]{0:T(128)} dynamic-slice(s32[256]{0:T(256)} %param.10, s32[]{:T(128)S(6)} %select_n.3), dynamic_slice_sizes={32} | dynamic-slice | bytes 260 | tf_op jit(solution)/shard_map/dynamic_slice | solution.py:336
  1.3 13.3 %spectra.1.d_ref = f32[2,128,32,128]{3,2,1,0:T(8,128)} custom-call(s32[32]{0:T(128)} %dynamic_slice.3.code_ref, f32[4,2,128]{2,1,0:T(2,128)} %codes_ref.1, f32[2,256,128]{2,1,0:T(8,128)} %constant.18.clone.head_ref, f32[128,128]{1,0:T(8,128)} %constant.19.clone.tri_ref, f32[264,896]{1,0:T(8,128)} %constant.20.clone.body_ref, f32[32,64,1024]{2,1,0:T(8,128)} %x_ref.1), custom_call_target="tpu_custom_call" | custom-call | tf_op jit(solution)/shard_map/spectra/pallas_call | solution.py:99
  14.6 76.2 %beams.1 = f32[16,32,256]{2,1,0:T(8,128)} custom-call(s32[1,256]{1,0:T(1,128)} %bitcast.3, f32[2,128,32,128]{3,2,1,0:T(8,128)} %spectra.1.d_ref, f32[16,16,64,256]{3,2,1,0:T(8,128)} %bitcast.2), custom_call_target="tpu_custom_call" | custom-call | tf_op jit(solution)/shard_map/beams/pallas_call | solution.py:306
  90.8 1.9 %copy.10 = f32[16,32,256]{2,1,0:T(8,128)} copy(f32[16,32,256]{2,1,0:T(8,128)} %beams.1) | data formatting | bytes 1048576

commit v3 on v2

v3 whole, which is shorter than its diff:
```python
import functools

import numpy as np
import jax
import jax.numpy as jnp
from jax import lax
from jax.experimental import pallas as pl
from jax.experimental.pallas import tpu as pltpu
from jax.sharding import PartitionSpec as P

HIGH = lax.Precision.HIGH
NT = (((1,), (1,)), ((), ()))
MESH = pl.DeviceIdType.MESH
ROUNDS = 16
LAG_B, LAG_C, LAG_D, LAG_E = 1, 3, 5, 7
SLOTS = 8
SLOT_Y = (2, 1, 2, 3, 1, 3, 0, 0)
SLOT_X = (0, 1, 1, 0, 0, 1, 0, 1)
RESIDUES = ((0, 8, 1, 15, 2, 14, 3, 13), (4, 12, 5, 11, 6, 10, 7, 9))
EBLK = 8
QUART = 64


def dft_tables(samples, taps):
    t = np.arange(taps, samples)
    u = np.arange(taps)
    bodies, heads = [], []
    for g in range(2):
        freq = (16 * np.arange(8)[:, None] + np.array(RESIDUES[g])[None, :]).reshape(-1)
        angle = 2 * np.pi * (freq[:, None] * t[None] % samples) / samples
        cosine, sine, extra = np.cos(angle), np.sin(angle), np.zeros((8, t.size))
        if g == 0:
            top = 2 * np.pi * (128 * t % samples) / samples
            sine[0], extra[0] = np.cos(top), np.sin(top)
        bodies.append(np.concatenate([cosine, sine, extra], 0))
        both = np.concatenate([freq, np.where(freq == 0, -128, -freq)])
        angle = 2 * np.pi * (both[:, None] * u[None] % samples) / samples
        heads.append(np.stack([np.cos(angle), np.sin(angle)]))
    tri = (u[:, None] <= u[None, :]).astype(np.float32)
    return np.stack(bodies).astype(np.float32), np.stack(heads).astype(np.float32), tri


def fill_tables(g, codes_ref, head_ref, tri_ref, gain_ref, tab_ref, scale):
    ncode, _, taps = codes_ref.shape
    cosine, sine = head_ref[g, 0], head_ref[g, 1]
    nrow = 2 * QUART
    for c in range(ncode):
        ci = codes_ref[c, 0:1, :] * scale
        cq = codes_ref[c, 1:2, :] * scale
        a_re = ci * cosine - cq * sine
        a_im = ci * sine + cq * cosine
        p_re = jnp.dot(a_re, tri_ref[...], precision=HIGH, preferred_element_type=jnp.float32)
        p_im = jnp.dot(a_im, tri_ref[...], precision=HIGH, preferred_element_type=jnp.float32)
        lanes = slice(c * taps, (c + 1) * taps)
        gain_ref[g, 0:nrow, lanes] = cosine * p_re + sine * p_im
        gain_ref[g, nrow:, lanes] = cosine * p_im - sine * p_re
        tab_ref[g, c, 0:nrow] = jnp.broadcast_to(p_re[:, taps - 1:], (nrow, 128))
        tab_ref[g, c, nrow:] = jnp.broadcast_to(p_im[:, taps - 1:], (nrow, 128))


def transform(g, blk, first_code, code_ref, x_ref, body_ref, gain_ref, tab_ref, spec_ref):
    _, mdev, samples = x_ref.shape
    ncode, taps = tab_ref.shape[1], gain_ref.shape[2] // tab_ref.shape[1]
    nrow = 2 * QUART
    start = pl.multiple_of(blk * EBLK, EBLK)
    x = x_ref[pl.ds(start, EBLK)].reshape(EBLK * mdev, samples)
    spec = lax.dot_general(body_ref[g], x[:, taps:], NT, precision=HIGH, preferred_element_type=jnp.float32)
    codes = [code_ref[first_code + start + e] for e in range(EBLK)]
    masked = jnp.concatenate(
        [
            jnp.concatenate(
                [x_ref[start + e, :, 0:taps] * (codes[e] == c).astype(jnp.float32) for e in range(EBLK)], axis=0
            )
            for c in range(ncode)
        ],
        axis=1,
    )
    corr = lax.dot_general(gain_ref[g], masked, NT, precision=HIGH, preferred_element_type=jnp.float32)
    first = lax.broadcasted_iota(jnp.int32, (QUART, 128), 0) == 0
    left = lax.broadcasted_iota(jnp.int32, (QUART, 128), 1) < mdev
    for sign in range(2):
        rows = slice(sign * QUART, (sign + 1) * QUART)
        irows = slice(nrow + sign * QUART, nrow + (sign + 1) * QUART)
        planes = []
        for q in range(EBLK // 2):
            lanes = slice(q * 128, (q + 1) * 128)
            xc, xs = spec[0:QUART, lanes], spec[QUART:nrow, lanes]
            cr = jnp.where(left, tab_ref[g, codes[2 * q], rows], tab_ref[g, codes[2 * q + 1], rows])
            ci = jnp.where(left, tab_ref[g, codes[2 * q], irows], tab_ref[g, codes[2 * q + 1], irows])
            if sign == 0:
                xs = jnp.where(first, 0.0, -xs) if g == 0 else -xs
            elif g == 0:
                xc = jnp.where(first, xs, xc)
                xs = jnp.where(first, spec[nrow:nrow + 1, lanes], xs)
            re = xc * cr - xs * ci + corr[rows, lanes]
            im = xc * ci + xs * cr + corr[irows, lanes]
            planes.append(jnp.where(left, re, pltpu.roll(im, 64, 1)))
            planes.append(jnp.where(left, pltpu.roll(re, 64, 1), im))
        spec_ref[g, sign, :, pl.ds(start, EBLK), :] = jnp.swapaxes(jnp.stack(planes, 0), 0, 1)


def beam_kernel(
    code_ref, codes_hbm, head_hbm, tri_hbm, body_hbm, order_hbm, traces_ref, steer_ref, out_ref,
    codes_ref, head_ref, tri_ref, body_ref, order_ref, xbuf, gain, tab, spec, wbuf, sendc, recvc, acc, recv1, recv2, fwd, totx, recvx, fin, gath, dec, had,
    tsem, wsem, csem, crsem, ysem, yrsem, y2sem, y2rsem, xsem, xrsem, asem, arsem, osem, orsem, ksem,
):
    i, j = lax.axis_index("emit"), lax.axis_index("elem")
    y, x, c = j // 4, j // 2 % 2, j % 2
    nemit = 8
    edev, mdev, samples = xbuf.shape
    lines = steer_ref.shape[3] // 2
    own_rows = pl.ds(pl.multiple_of(i * edev, edev), edev)

    def at(yy, xx, cc):
        return (i, (yy * 2 + xx) * 2 + cc)

    other_core = at(y, x, 1 - c)
    up, down = at((y + 1) % 4, x, c), at((y + 3) % 4, x, c)
    other_x = at(y, 1 - x, c)

    def emit_peer(q):
        return ((i + q) % nemit, j)

    def member(t):
        return (i + t) % nemit

    def bin_in_block(g, n):
        u, w = 4 * g + n // 2, n % 2
        return u * (1 - w) + w * (16 - u - 8 * (1 - (u + 7) // 8))

    def remote(src, dst, ssem, rsem, device):
        return pltpu.make_async_remote_copy(
            src_ref=src, dst_ref=dst, send_sem=ssem, recv_sem=rsem, device_id=device, device_id_type=MESH
        )

    def load(t):
        return pltpu.make_async_copy(
            steer_ref.at[:, bin_in_block(t // 8, member(t))], wbuf.at[t % SLOTS], wsem.at[t % SLOTS]
        )

    def load_traces(blk):
        part = pl.ds(blk * EBLK, EBLK)
        return pltpu.make_async_copy(traces_ref.at[part], xbuf.at[part], tsem.at[blk])

    def core_copy(t):
        return remote(sendc.at[t], recvc.at[t], csem.at[t], crsem.at[t], other_core)

    def y1_copy(t, d):
        return remote(acc.at[t, pl.ds(2 * d, 2)], recv1.at[t, d], ysem.at[t, d], yrsem.at[t, d], up if d == 0 else down)

    def y2_copy(t, d):
        return remote(fwd.at[t, d], recv2.at[t, d], y2sem.at[t, d], y2rsem.at[t, d], up if d == 0 else down)

    def x_copy(t):
        return remote(totx.at[t], recvx.at[t], xsem.at[t], xrsem.at[t], other_x)

    def a_copy(t):
        return remote(fin.at[t], gath.at[t // nemit, own_rows], asem.at[t], arsem.at[t], emit_peer(t))

    def rows_of(q):
        return pl.ds(pl.multiple_of((i + q) % nemit * edev, edev), edev)

    def o_copy(s, q):
        return remote(dec.at[s, rows_of(q)], out_ref.at[bin_in_block(s, i)], osem.at[s, q], orsem.at[s, q], emit_peer(q))

    nblk = edev // EBLK
    pairs = [
        (codes_hbm, codes_ref), (tri_hbm, tri_ref), (head_hbm, head_ref), (body_hbm.at[0], body_ref.at[0]),
        (body_hbm.at[1], body_ref.at[1]), (order_hbm, order_ref),
    ]
    tables = [pltpu.make_async_copy(a, b, ksem.at[n]) for n, (a, b) in enumerate(pairs)]
    for table in tables[:4]:
        table.start()
    for blk in range(nblk):
        load_traces(blk).start()
    for table in tables[4:]:
        table.start()
    for t in range(6):
        load(t).start()
    barrier = pltpu.get_barrier_semaphore()
    peers = [other_core, up, down, other_x] + [emit_peer(q) for q in range(1, nemit)]
    for peer in peers:
        pl.semaphore_signal(barrier, inc=1, device_id=peer, device_id_type=MESH)

    scale = float(samples) ** -0.5
    for table in tables[:3]:
        table.wait()
    for g in range(2):
        fill_tables(g, codes_ref, head_ref, tri_ref, gain, tab, scale)
    tables[3].wait()

    def first_half(blk, carry):
        load_traces(blk).wait()
        transform(0, blk, i * edev, code_ref, xbuf, body_ref, gain, tab, spec)
        return carry

    lax.fori_loop(0, nblk, first_half, 0)
    pl.semaphore_wait(barrier, len(peers))
    tables[4].wait()

    def product(t, slot, core):
        jj = ((y + SLOT_Y[slot]) % 4 * 2 + SLOT_X[slot]) * 2 + core
        g, n = t // 8, member(t)
        neg = 1 - jj // 8
        whole = 8 * g + n
        flip = (whole + 14) // 16 * (1 - 2 * (n % 2))
        row_pos = (jj - 8 * (1 - neg)) * 8 + n
        row_neg = (16 - jj - (whole + 15) // 16) % 8 * 8 + n + flip
        row = (1 - neg) * row_pos + neg * row_neg
        s = wbuf[t % SLOTS, jj]
        w = jnp.concatenate([s, jnp.concatenate([-s[:, lines:], s[:, :lines]], axis=1)], axis=0)
        return jnp.dot(spec[g, neg, row], w, precision=HIGH, preferred_element_type=jnp.float32)

    def twice(h, data):
        hi = data.astype(jnp.bfloat16)
        lo = (data - hi.astype(jnp.float32)).astype(jnp.bfloat16)
        return jnp.dot(h, hi, preferred_element_type=jnp.float32) + jnp.dot(h, lo, preferred_element_type=jnp.float32)

    def decode(s):
        for q in range(1, nemit):
            a_copy(s * nemit + q).wait_recv()
        dec[s] = twice(had[...], gath[s])
        for q in range(1, nemit):
            o_copy(s, q).start()
        out_ref[bin_in_block(s, i)] = dec[s, own_rows]

    def body(t, carry):
        @pl.when(t + 5 < ROUNDS)
        def _():
            @pl.when(t >= 1)
            def _():
                load(t + 5).start()

        @pl.when(t < ROUNDS)
        def _():
            load(t).wait()
            for slot in range(8):
                sendc[t, slot] = product(t, slot, 1 - c)
            core_copy(t).start()

        @pl.when((t >= LAG_B) & (t < ROUNDS + LAG_B))
        def _():
            u = t - LAG_B
            core_copy(u).wait_recv()
            for slot in range(8):
                acc[u, slot] = product(u, slot, c) + recvc[u, slot]
                if slot == 1:
                    y1_copy(u, 0).start()
                if slot == 3:
                    y1_copy(u, 1).start()

        @pl.when((t >= LAG_C) & (t < ROUNDS + LAG_C))
        def _():
            u = t - LAG_C
            for d in range(2):
                y1_copy(u, d).wait_recv()
                fwd[u, d] = acc[u, 4 + d] + recv1[u, d, 0]
                y2_copy(u, d).start()

        @pl.when((t >= LAG_D) & (t < ROUNDS + LAG_D))
        def _():
            u = t - LAG_D
            for d in range(2):
                y2_copy(u, d).wait_recv()
            tot0 = acc[u, 6] + recv2[u, 0] + recv1[u, 1, 1]
            tot1 = acc[u, 7] + recv2[u, 1] + recv1[u, 0, 1]
            totx[u] = jnp.where(x == 0, tot1, tot0)
            fin[u] = jnp.where(x == 0, tot0, tot1)
            x_copy(u).start()

        @pl.when((t >= LAG_E) & (t < ROUNDS + LAG_E))
        def _():
            u = t - LAG_E
            x_copy(u).wait_recv()
            fin[u] = fin[u] + recvx[u]

            @pl.when(u % nemit == 0)
            def _():
                gath[u // nemit, own_rows] = fin[u]

            @pl.when(u % nemit != 0)
            def _():
                a_copy(u).start()

        @pl.when(t == nemit + LAG_E + 2)
        def _():
            decode(0)

        @pl.when((t < 2 * nblk) & (t % 2 == 1))
        def _():
            transform(1, t // 2, i * edev, code_ref, xbuf, body_ref, gain, tab, spec)

        @pl.when(t == 9)
        def _():
            tables[5].wait()
            both = order_ref[...] & lax.broadcasted_iota(jnp.int32, had.shape, 0)
            for shift in (4, 2, 1):
                both = both ^ (both >> shift)
            had[...] = ((1 - 2 * (both & 1)).astype(jnp.float32) * (had.shape[0] ** -0.5)).astype(jnp.bfloat16)

        return carry

    lax.fori_loop(0, ROUNDS + LAG_E, body, 0)

    decode(1)

    def drain(t, carry):
        core_copy(t).wait_send()
        for d in range(2):
            y1_copy(t, d).wait_send()
            y2_copy(t, d).wait_send()
        x_copy(t).wait_send()
        return carry

    lax.fori_loop(0, ROUNDS, drain, 0)
    for s in range(2):
        for q in range(1, nemit):
            a_copy(s * nemit + q).wait_send()
            o_copy(s, q).wait()


def per_device(traces, codes, code_of, order, steer):
    edev, mdev, samples = traces.shape
    ncode, _, taps = codes.shape
    bins, _, width = steer.shape
    emissions = order.shape[0]
    body, head, tri = dft_tables(samples, taps)
    f32 = jnp.float32
    block = (edev, width)
    dma = pltpu.SemaphoreType.DMA
    vmem = pl.BlockSpec(memory_space=pltpu.VMEM)
    hbm = pl.BlockSpec(memory_space=pl.ANY)
    return pl.pallas_call(
        beam_kernel,
        in_specs=[pl.BlockSpec(memory_space=pltpu.SMEM), hbm, hbm, hbm, hbm, hbm, hbm, hbm],
        out_specs=vmem,
        out_shape=jax.ShapeDtypeStruct((16, edev, width), f32),
        scratch_shapes=[
            pltpu.VMEM(codes.shape, f32),
            pltpu.VMEM(head.shape, f32),
            pltpu.VMEM(tri.shape, f32),
            pltpu.VMEM(body.shape, f32),
            pltpu.VMEM((1, emissions), jnp.int32),
            pltpu.VMEM(traces.shape, f32),
            pltpu.VMEM((2, 4 * QUART, ncode * taps), f32),
            pltpu.VMEM((2, ncode, 4 * QUART, 128), f32),
            pltpu.VMEM((2, 2, QUART, edev, 2 * mdev), f32),
            pltpu.VMEM((SLOTS, 16, mdev, width), f32),
            pltpu.VMEM((ROUNDS, 8) + block, f32),
            pltpu.VMEM((ROUNDS, 8) + block, f32),
            pltpu.VMEM((ROUNDS, 8) + block, f32),
            pltpu.VMEM((ROUNDS, 2, 2) + block, f32),
            pltpu.VMEM((ROUNDS, 2) + block, f32),
            pltpu.VMEM((ROUNDS, 2) + block, f32),
            pltpu.VMEM((ROUNDS,) + block, f32),
            pltpu.VMEM((ROUNDS,) + block, f32),
            pltpu.VMEM((ROUNDS,) + block, f32),
            pltpu.VMEM((2, emissions, width), f32),
            pltpu.VMEM((2, emissions, width), f32),
            pltpu.VMEM((emissions, emissions), jnp.bfloat16),
            dma((edev // EBLK,)), dma((SLOTS,)), dma((ROUNDS,)), dma((ROUNDS,)),
            dma((ROUNDS, 2)), dma((ROUNDS, 2)), dma((ROUNDS, 2)), dma((ROUNDS, 2)),
            dma((ROUNDS,)), dma((ROUNDS,)), dma((ROUNDS,)), dma((ROUNDS,)), dma((2, 8)), dma((2, 8)), dma((6,)),
        ],
        compiler_params=pltpu.CompilerParams(collective_id=0, has_side_effects=True, vmem_limit_bytes=60 << 20),
        name="beams",
    )(
        code_of, codes, head, tri, body, order.reshape(1, emissions), traces,
        steer.reshape(16, bins // 16, mdev, width),
    )


def solution(mesh):
    placed = (P("emit", "elem", None), P(), P(), P(), P(None, "elem", None))
    return jax.shard_map(
        per_device, mesh=mesh, in_specs=placed, out_specs=P("elem", "emit", None), check_vma=False
    )
```

time: 92.9 us -> 75.3 us (0.81)
  Pallas kernels: 89.6 us -> 73.2 us
  local copies, waits for them, and re-layouts: 3.14 us -> 1.88 us
    pallas_call x2 -> x1, Pallas kernels: 89.6 us -> 73.2 us  [per_device(): pl.pallas_call(beam_kernel, in_specs=[pl.BlockSpec(memory_space=pltpu.SME...]
    dynamic_slice x1 -> x0, local copies, waits for them, and re-layouts: 1.26 us -> none  [per_device(): own_codes = lax.dynamic_slice_in_dim(code_of, first, edev)]
where the time goes in v3:
time: 75.3 us; the launch traced here: 75.1 us
  Pallas kernels  73.2 us (97%)
  local copies, waits for them, and re-layouts  1.88 us (2%)
    pallas_call x1, Pallas kernels, per_device(): pl.pallas_call(beam_kernel, in_specs=[pl.BlockSpec(memory_space=pltpu.SME...  73.2 us
    unnamed x1, local copies, waits for them, and re-layouts  1.88 us

profile of v3, /device:TPU:0, one launch (start us, length us, event | category | flops | bytes accessed | tf_op | source)
XLA Modules:
  0.0 75.1 jit_solution(12911527807840350122)
XLA Ops:
  0.0 73.2 %beams.1 = f32[16,32,256]{2,1,0:T(8,128)} custom-call(s32[256]{0:T(256)} %code_ref.1, f32[4,2,128]{2,1,0:T(2,128)} %codes_hbm.1, f32[2,2,128,128]{3,2,1,0:T(8,128)} %constant.6.clone.head_hbm, f32[128,128]{1,0:T(8,128)} %constant.7.clone.tri_hbm, f32[2,136,896]{2,1,0:T(8,128)} %constant.8.clone.body_hbm, s32[1,256]{1,0:T(1,128)} %bitcast.3, ...), custom_call_target="tpu_custom_call" | custom-call | tf_op jit(solution)/shard_map/beams/pallas_call | solution.py:333
  73.3 1.9 %copy.10 = f32[16,32,256]{2,1,0:T(8,128)} copy(f32[16,32,256]{2,1,0:T(8,128)} %beams.1) | data formatting | bytes 1048576

commit v4 on v3

--- a/solution.py
+++ b/solution.py
@@ -12,6 +12,8 @@
 NT = (((1,), (1,)), ((), ()))
 MESH = pl.DeviceIdType.MESH
 ROUNDS = 16
+FLIPS = 3
+FAR_FIRST = (2, 6, 3, 5, 4, 1, 7)
 LAG_B, LAG_C, LAG_D, LAG_E = 1, 3, 5, 7
 SLOTS = 8
 SLOT_Y = (2, 1, 2, 3, 1, 3, 0, 0)
@@ -101,13 +103,15 @@
 
 def beam_kernel(
     code_ref, codes_hbm, head_hbm, tri_hbm, body_hbm, order_hbm, traces_ref, steer_ref, out_ref,
-    codes_ref, head_ref, tri_ref, body_ref, order_ref, xbuf, gain, tab, spec, wbuf, sendc, recvc, acc, recv1, recv2, fwd, totx, recvx, fin, gath, dec, had,
+    codes_ref, head_ref, tri_ref, body_ref, order_ref, xbuf, gain, tab, spec, wbuf, sendc, recvc, acc, recv1, recv2, fwd, totx, recvx, fin, gath, dec, had, frecv, facc, frecv1, ffwd, frecv2,
     tsem, wsem, csem, crsem, ysem, yrsem, y2sem, y2rsem, xsem, xrsem, asem, arsem, osem, orsem, ksem,
+    fsem, frsem, f1sem, f1rsem, f2sem, f2rsem,
 ):
     i, j = lax.axis_index("emit"), lax.axis_index("elem")
     y, x, c = j // 4, j // 2 % 2, j % 2
     nemit = 8
     edev, mdev, samples = xbuf.shape
+    hrow = edev // 2
     lines = steer_ref.shape[3] // 2
     own_rows = pl.ds(pl.multiple_of(i * edev, edev), edev)
 
@@ -153,6 +157,19 @@
 
     def x_copy(t):
         return remote(totx.at[t], recvx.at[t], xsem.at[t], xrsem.at[t], other_x)
+
+    def flipped(t):
+        return (t % 4 == 3) & (t < 4 * FLIPS)
+
+    def f_copy(w):
+        t = 4 * w + 3
+        return remote(acc.at[t, pl.ds(pl.multiple_of((1 - x) * 4, 4), 4)], frecv.at[w], fsem.at[w], frsem.at[w], other_x)
+
+    def f1_copy(w, d):
+        return remote(facc.at[w, pl.ds(2 * d, 2)], frecv1.at[w, d], f1sem.at[w, d], f1rsem.at[w, d], up if d == 0 else down)
+
+    def f2_copy(w, d):
+        return remote(ffwd.at[w, d], frecv2.at[w, d], f2sem.at[w, d], f2rsem.at[w, d], up if d == 0 else down)
 
     def a_copy(t):
         return remote(fin.at[t], gath.at[t // nemit, own_rows], asem.at[t], arsem.at[t], emit_peer(t))
@@ -220,7 +237,7 @@
         for q in range(1, nemit):
             a_copy(s * nemit + q).wait_recv()
         dec[s] = twice(had[...], gath[s])
-        for q in range(1, nemit):
+        for q in FAR_FIRST:
             o_copy(s, q).start()
         out_ref[bin_in_block(s, i)] = dec[s, own_rows]
 
@@ -242,37 +259,80 @@
         def _():
             u = t - LAG_B
             core_copy(u).wait_recv()
-            for slot in range(8):
-                acc[u, slot] = product(u, slot, c) + recvc[u, slot]
-                if slot == 1:
-                    y1_copy(u, 0).start()
-                if slot == 3:
-                    y1_copy(u, 1).start()
+
+            @pl.when(~flipped(u))
+            def _():
+                for slot in range(8):
+                    acc[u, slot] = product(u, slot, c) + recvc[u, slot]
+                    if slot == 1 or slot == 3:
+                        y1_copy(u, slot // 2).start()
+
+            @pl.when(flipped(u))
+            def _():
+                for slot in range(8):
+                    acc[u, SLOT_X[slot] * 4 + SLOT_Y[slot]] = product(u, slot, c) + recvc[u, slot]
+                f_copy(u // 4).start()
 
         @pl.when((t >= LAG_C) & (t < ROUNDS + LAG_C))
         def _():
             u = t - LAG_C
-            for d in range(2):
-                y1_copy(u, d).wait_recv()
-                fwd[u, d] = acc[u, 4 + d] + recv1[u, d, 0]
-                y2_copy(u, d).start()
+            w = u // 4
+
+            @pl.when(~flipped(u))
+            def _():
+                for d in range(2):
+                    y1_copy(u, d).wait_recv()
+                    fwd[u, d] = acc[u, 4 + d] + recv1[u, d, 0]
+                    y2_copy(u, d).start()
+
+            @pl.when(flipped(u))
+            def _():
+                f_copy(w).wait_recv()
+                for slot in range(8):
+                    rows = slice(SLOT_X[slot] * hrow, (SLOT_X[slot] + 1) * hrow)
+                    facc[w, slot] = acc[u, x * 4 + SLOT_Y[slot], rows] + frecv[w, SLOT_Y[slot], rows]
+                    if slot == 1 or slot == 3:
+                        f1_copy(w, slot // 2).start()
 
         @pl.when((t >= LAG_D) & (t < ROUNDS + LAG_D))
         def _():
             u = t - LAG_D
-            for d in range(2):
-                y2_copy(u, d).wait_recv()
-            tot0 = acc[u, 6] + recv2[u, 0] + recv1[u, 1, 1]
-            tot1 = acc[u, 7] + recv2[u, 1] + recv1[u, 0, 1]
-            totx[u] = jnp.where(x == 0, tot1, tot0)
-            fin[u] = jnp.where(x == 0, tot0, tot1)
-            x_copy(u).start()
+            w = u // 4
+
+            @pl.when(~flipped(u))
+            def _():
+                for d in range(2):
+                    y2_copy(u, d).wait_recv()
+                tot0 = acc[u, 6] + recv2[u, 0] + recv1[u, 1, 1]
+                tot1 = acc[u, 7] + recv2[u, 1] + recv1[u, 0, 1]
+                totx[u] = jnp.where(x == 0, tot1, tot0)
+                fin[u] = jnp.where(x == 0, tot0, tot1)
+                x_copy(u).start()
+
+            @pl.when(flipped(u))
+            def _():
+                for d in range(2):
+                    f1_copy(w, d).wait_recv()
+                    ffwd[w, d] = facc[w, 4 + d] + frecv1[w, d, 0]
+                    f2_copy(w, d).start()
 
         @pl.when((t >= LAG_E) & (t < ROUNDS + LAG_E))
         def _():
             u = t - LAG_E
-            x_copy(u).wait_recv()
-            fin[u] = fin[u] + recvx[u]
+            w = u // 4
+
+            @pl.when(~flipped(u))
+            def _():
+                x_copy(u).wait_recv()
+                fin[u] = fin[u] + recvx[u]
+
+            @pl.when(flipped(u))
+            def _():
+                for d in range(2):
+                    f2_copy(w, d).wait_recv()
+                fin[u, 0:hrow] = facc[w, 6] + frecv2[w, 0] + frecv1[w, 1, 1]
+                fin[u, hrow:] = facc[w, 7] + frecv2[w, 1] + frecv1[w, 0, 1]
+
 
             @pl.when(u % nemit == 0)
             def _():
@@ -306,13 +366,22 @@
 
     def drain(t, carry):
         core_copy(t).wait_send()
+
+        @pl.when(~flipped(t))
+        def _():
+            for d in range(2):
+                y1_copy(t, d).wait_send()
+                y2_copy(t, d).wait_send()
+            x_copy(t).wait_send()
+
+        return carry
+
+    lax.fori_loop(0, ROUNDS, drain, 0)
+    for w in range(FLIPS):
+        f_copy(w).wait_send()
         for d in range(2):
-            y1_copy(t, d).wait_send()
-            y2_copy(t, d).wait_send()
-        x_copy(t).wait_send()
-        return carry
-
-    lax.fori_loop(0, ROUNDS, drain, 0)
+            f1_copy(w, d).wait_send()
+            f2_copy(w, d).wait_send()
     for s in range(2):
         for q in range(1, nemit):
             a_copy(s * nemit + q).wait_send()
@@ -326,7 +395,7 @@
     emissions = order.shape[0]
     body, head, tri = dft_tables(samples, taps)
     f32 = jnp.float32
-    block = (edev, width)
+    block, halved = (edev, width), (edev // 2, width)
     dma = pltpu.SemaphoreType.DMA
     vmem = pl.BlockSpec(memory_space=pltpu.VMEM)
     hbm = pl.BlockSpec(memory_space=pl.ANY)
@@ -358,9 +427,15 @@
             pltpu.VMEM((2, emissions, width), f32),
             pltpu.VMEM((2, emissions, width), f32),
             pltpu.VMEM((emissions, emissions), jnp.bfloat16),
+            pltpu.VMEM((FLIPS, 4) + block, f32),
+            pltpu.VMEM((FLIPS, 8) + halved, f32),
+            pltpu.VMEM((FLIPS, 2, 2) + halved, f32),
+            pltpu.VMEM((FLIPS, 2) + halved, f32),
+            pltpu.VMEM((FLIPS, 2) + halved, f32),
             dma((edev // EBLK,)), dma((SLOTS,)), dma((ROUNDS,)), dma((ROUNDS,)),
             dma((ROUNDS, 2)), dma((ROUNDS, 2)), dma((ROUNDS, 2)), dma((ROUNDS, 2)),
             dma((ROUNDS,)), dma((ROUNDS,)), dma((ROUNDS,)), dma((ROUNDS,)), dma((2, 8)), dma((2, 8)), dma((6,)),
+            dma((FLIPS,)), dma((FLIPS,)), dma((FLIPS, 2)), dma((FLIPS, 2)), dma((FLIPS, 2)), dma((FLIPS, 2)),
         ],
         compiler_params=pltpu.CompilerParams(collective_id=0, has_side_effects=True, vmem_limit_bytes=60 << 20),
         name="beams",

time: 75.3 us -> 74.4 us (0.988)
  Pallas kernels: 73.2 us -> 72.4 us
    pallas_call x1, Pallas kernels: 73.2 us -> 72.4 us  [per_device(): pl.pallas_call(beam_kernel, in_specs=[pl.BlockSpec(memory_space=pltpu.SME...]
where the time goes in v4:
time: 74.4 us; the launch traced here: 74.3 us
  Pallas kernels  72.4 us (97%)
  local copies, waits for them, and re-layouts  1.88 us (3%)
    pallas_call x1, Pallas kernels, per_device(): pl.pallas_call(beam_kernel, in_specs=[pl.BlockSpec(memory_space=pltpu.SME...  72.4 us
    unnamed x1, local copies, waits for them, and re-layouts  1.88 us

profile of v4, /device:TPU:0, one launch (start us, length us, event | category | flops | bytes accessed | tf_op | source)
XLA Modules:
  0.0 74.3 jit_solution(4963156784719014406)
XLA Ops:
  0.0 72.4 %beams.1 = f32[16,32,256]{2,1,0:T(8,128)} custom-call(s32[256]{0:T(256)} %code_ref.1, f32[4,2,128]{2,1,0:T(2,128)} %codes_hbm.1, f32[2,2,128,128]{3,2,1,0:T(8,128)} %constant.6.clone.head_hbm, f32[128,128]{1,0:T(8,128)} %constant.7.clone.tri_hbm, f32[2,136,896]{2,1,0:T(8,128)} %constant.8.clone.body_hbm, s32[1,256]{1,0:T(1,128)} %bitcast.3, ...), custom_call_target="tpu_custom_call" | custom-call | tf_op jit(solution)/shard_map/beams/pallas_call | solution.py:402
  72.4 1.9 %copy.10 = f32[16,32,256]{2,1,0:T(8,128)} copy(f32[16,32,256]{2,1,0:T(8,128)} %beams.1) | data formatting | bytes 1048576

commit v5 on v4

--- a/solution.py
+++ b/solution.py
@@ -225,8 +225,16 @@
         row_neg = (16 - jj - (whole + 15) // 16) % 8 * 8 + n + flip
         row = (1 - neg) * row_pos + neg * row_neg
         s = wbuf[t % SLOTS, jj]
-        w = jnp.concatenate([s, jnp.concatenate([-s[:, lines:], s[:, :lines]], axis=1)], axis=0)
-        return jnp.dot(spec[g, neg, row], w, precision=HIGH, preferred_element_type=jnp.float32)
+        d = spec[g, neg, row]
+        w_hi = s.astype(jnp.bfloat16)
+        w_lo = (s - w_hi.astype(jnp.float32)).astype(jnp.bfloat16)
+        d_hi = d.astype(jnp.bfloat16)
+        d_lo = (d - d_hi.astype(jnp.float32)).astype(jnp.bfloat16)
+        turn = lambda v: jnp.concatenate([-v[:, lines:], v[:, :lines]], axis=1)
+        left = jnp.concatenate([jnp.concatenate([d_hi, d_hi], axis=1), jnp.concatenate([d_lo, jnp.zeros_like(d_lo)], axis=1)], axis=0)
+        right = jnp.concatenate([w_hi, turn(w_hi), w_lo, turn(w_lo)], axis=0)
+        both = jnp.dot(left, right, preferred_element_type=jnp.float32)
+        return both[:edev] + both[edev:]
 
     def twice(h, data):
         hi = data.astype(jnp.bfloat16)

time: 74.4 us -> 74 us (level)
  no operation moved by 1% of the time
where the time goes in v5:
time: 74 us; the launch traced here: 73.8 us
  Pallas kernels  72 us (97%)
  local copies, waits for them, and re-layouts  1.88 us (3%)
    pallas_call x1, Pallas kernels, per_device(): pl.pallas_call(beam_kernel, in_specs=[pl.BlockSpec(memory_space=pltpu.SME...  72 us
    unnamed x1, local copies, waits for them, and re-layouts  1.88 us

profile of v5, /device:TPU:0, one launch (start us, length us, event | category | flops | bytes accessed | tf_op | source)
XLA Modules:
  0.0 73.8 jit_solution(11732647076920306746)
XLA Ops:
  0.0 72.0 %beams.1 = f32[16,32,256]{2,1,0:T(8,128)} custom-call(s32[256]{0:T(256)} %code_ref.1, f32[4,2,128]{2,1,0:T(2,128)} %codes_hbm.1, f32[2,2,128,128]{3,2,1,0:T(8,128)} %constant.6.clone.head_hbm, f32[128,128]{1,0:T(8,128)} %constant.7.clone.tri_hbm, f32[2,136,896]{2,1,0:T(8,128)} %constant.8.clone.body_hbm, s32[1,256]{1,0:T(1,128)} %bitcast.3, ...), custom_call_target="tpu_custom_call" | custom-call | tf_op jit(solution)/shard_map/beams/pallas_call | solution.py:410
  72.0 1.9 %copy.10 = f32[16,32,256]{2,1,0:T(8,128)} copy(f32[16,32,256]{2,1,0:T(8,128)} %beams.1) | data formatting | bytes 1048576

commit v6 on v5

--- a/solution.py
+++ b/solution.py
@@ -354,9 +354,9 @@
         def _():
             decode(0)
 
-        @pl.when((t < 2 * nblk) & (t % 2 == 1))
-        def _():
-            transform(1, t // 2, i * edev, code_ref, xbuf, body_ref, gain, tab, spec)
+        @pl.when((t >= 2) & (t < 8) & (t != 3) & (t != 6))
+        def _():
+            transform(1, (t - 1) // 2, i * edev, code_ref, xbuf, body_ref, gain, tab, spec)
 
         @pl.when(t == 9)
         def _():

time: 74 us -> 73.6 us (level)
  no operation moved by 1% of the time
where the time goes in v6:
time: 73.6 us; the launch traced here: 73.4 us
  Pallas kernels  71.5 us (97%)
  local copies, waits for them, and re-layouts  1.88 us (3%)
    pallas_call x1, Pallas kernels, per_device(): pl.pallas_call(beam_kernel, in_specs=[pl.BlockSpec(memory_space=pltpu.SME...  71.5 us
    unnamed x1, local copies, waits for them, and re-layouts  1.88 us

profile of v6, /device:TPU:0, one launch (start us, length us, event | category | flops | bytes accessed | tf_op | source)
XLA Modules:
  0.0 73.4 jit_solution(2741119683012578306)
XLA Ops:
  0.0 71.5 %beams.1 = f32[16,32,256]{2,1,0:T(8,128)} custom-call(s32[256]{0:T(256)} %code_ref.1, f32[4,2,128]{2,1,0:T(2,128)} %codes_hbm.1, f32[2,2,128,128]{3,2,1,0:T(8,128)} %constant.6.clone.head_hbm, f32[128,128]{1,0:T(8,128)} %constant.7.clone.tri_hbm, f32[2,136,896]{2,1,0:T(8,128)} %constant.8.clone.body_hbm, s32[1,256]{1,0:T(1,128)} %bitcast.3, ...), custom_call_target="tpu_custom_call" | custom-call | tf_op jit(solution)/shard_map/beams/pallas_call | solution.py:410
  71.5 1.9 %copy.10 = f32[16,32,256]{2,1,0:T(8,128)} copy(f32[16,32,256]{2,1,0:T(8,128)} %beams.1) | data formatting | bytes 1048576
